TPU v7x, 32 devices: a whole 2x2x4 slice. The times are simulated.
32 devices in a mesh: blk: 4 (over y, x), grp: 8 (over z, core).
Axes of the slice: x: 2, y: 2, z: 4, core: 2. Of those that a mesh axis runs over, the one named last changes fastest.
Arguments:
- position: float32 [3, 8192], P(None, ('blk', 'grp'))
- velocity: float32 [3, 8192], P(None, ('blk', 'grp')), may hold values from -3 to 3
- accel_old: float32 [3, 8192], P(None, ('blk', 'grp')), may hold values from -5 to 5
- jerk_old: float32 [3, 8192], P(None, ('blk', 'grp')), may hold values from -5 to 5
- elapsed: float32 [8192], P(('blk', 'grp')), may hold values from 0.01 to 0.1
- masses: float32 [8192], P(('blk', 'grp'))
- active_stars: int32 [1024], P(('blk', 'grp')), may hold values from 0 to 255, as said below
- neighbour_list: int32 [32, 16], P(('blk', 'grp')), may hold values from 0 to 15, as said below
- neighbour_count: int32 [32], P(('blk', 'grp')), may hold values from 1 to 16, as said below
Outputs:
- regular: float32 [6, 1024], P(None, ('blk', 'grp'))
- irregular: float32 [6, 1024], P(None, ('blk', 'grp'))
- correction: float32 [6, 1024], P(None, ('blk', 'grp'))
Inputs may be any that keep to these rules, and one draw needn't show every extreme that they name: `active_stars`: the 32 entries of one device are distinct local indices of that device's stars, all inside one block of 128 of them. `neighbour_list`: row r lists neighbour blocks for the active stars of device r, numbered within r's group (2 blocks a device, devices in grp order). Its first neighbour_count[r] entries are distinct and ascending, at most 2 of them from one device, and include the block that holds r's active stars; later entries mean nothing. `neighbour_count`: in every group along blk some device lists 2 blocks of every device of its group.
All inputs are finite; a program needn't handle non-finite values.
Results may differ from a plain program's by a relative error of at most 0.0003.
Values sent between devices are 32-bit elements; how exact they have to be, the bound alone decides.
A program may use at most 64 MiB of HBM per device.

v0:
```python
import jax
import jax.numpy as jnp
from jax import lax
from jax.sharding import PartitionSpec as P

BLOCK = 128


soften_sq = 0.0001


def shifted(block, axis, distance):
    devices = range(lax.axis_size(axis))
    route = [((i - distance) % len(devices), i) for i in devices]
    return lax.ppermute(block, axis, route)


def pair_sums(targets, sources, weight):
    gap_x = sources[0][None, :] - targets[0][:, None]
    gap_y = sources[1][None, :] - targets[1][:, None]
    gap_z = sources[2][None, :] - targets[2][:, None]
    rel_x = sources[3][None, :] - targets[3][:, None]
    rel_y = sources[4][None, :] - targets[4][:, None]
    rel_z = sources[5][None, :] - targets[5][:, None]
    dist_sq = gap_x * gap_x + gap_y * gap_y + gap_z * gap_z + soften_sq
    inverse = lax.rsqrt(dist_sq)
    scaled = weight * (inverse * inverse * inverse)
    radial = 3.0 * (gap_x * rel_x + gap_y * rel_y + gap_z * rel_z) / dist_sq
    term_list = [
        gap_x,
        gap_y,
        gap_z,
        rel_x - radial * gap_x,
        rel_y - radial * gap_y,
        rel_z - radial * gap_z,
    ]
    return jnp.stack([jnp.sum(scaled * term, axis=1) for term in term_list])


def per_device(
    position,
    velocity,
    accel_old,
    jerk_old,
    elapsed,
    masses,
    active_stars,
    neighbour_list,
    neighbour_count,
):
    moved_pos = position + elapsed * (
        velocity + elapsed * (0.5 * accel_old + elapsed * jerk_old / 6.0)
    )
    turned = velocity + elapsed * (accel_old + 0.5 * elapsed * jerk_old)
    sources = jnp.concatenate([moved_pos, turned], axis=0)
    own_set = jnp.take(sources, active_stars, axis=1)
    act_dev = active_stars.shape[0]
    res_dev = position.shape[1]
    blk_dev = res_dev // BLOCK
    group_set = lax.all_gather(own_set, "grp", axis=1, tiled=True)
    all_lists, all_counts = (
        lax.all_gather(neighbour_list, "grp", axis=0, tiled=True),
        lax.all_gather(neighbour_count, "grp", axis=0, tiled=True),
    )
    blk_size = lax.axis_size("blk")
    my_index = lax.axis_index("grp")
    slot_total = all_lists.shape[1]
    in_list = jnp.arange(slot_total)[None, :] < all_counts[:, None]
    my_blocks = my_index * blk_dev + jnp.arange(blk_dev)
    listed = jnp.any(
        in_list[:, :, None] & (all_lists[:, :, None] == my_blocks[None, None, :]), axis=1
    )
    keep_home = 1.0 - listed.astype(jnp.float32)
    keep_all = jnp.ones_like(keep_home)
    set_size = group_set.shape[1]
    piece_rows = min(512, set_size)
    piece_count = set_size // piece_rows
    owners_piece = piece_rows // act_dev
    moving = group_set
    running = jnp.zeros((6, set_size), jnp.float32)
    for step in range(blk_size):
        target_pieces = moving.reshape(6, piece_count, piece_rows).transpose(1, 0, 2)
        keep_pieces = (keep_home if step == 0 else keep_all).reshape(
            piece_count, owners_piece, blk_dev
        )

        def one_piece(items):
            target_piece, keep_piece = items
            weight = (
                jnp.repeat(jnp.repeat(keep_piece, act_dev, axis=0), BLOCK, axis=1) * masses[None, :]
            )
            return pair_sums(target_piece, sources, weight)

        sums = lax.map(one_piece, (target_pieces, keep_pieces))
        running = running + sums.transpose(1, 0, 2).reshape(6, set_size)
        moving, running = shifted((moving, running), "blk", 1)
    regular = lax.psum_scatter(running, "grp", scatter_dimension=1, tiled=True)
    block_data = jnp.concatenate([sources, masses[None, :]], axis=0).reshape(7, blk_dev, BLOCK)
    own_list = neighbour_list[0]
    own_live = jnp.arange(slot_total) < neighbour_count[0]
    everyone = lax.all_gather(block_data, "grp", axis=1, tiled=True)
    picked = jnp.take(everyone, own_list, axis=1)
    near_src = picked[:6].reshape(6, -1)
    near_mass = (picked[6] * own_live[:, None].astype(jnp.float32)).reshape(1, -1)
    irregular = pair_sums(own_set, near_src, near_mass)
    accel_now = regular[:3] + irregular[:3]
    jerk_now = regular[3:] + irregular[3:]
    step_time = jnp.take(elapsed, active_stars)
    start_accel = jnp.take(accel_old, active_stars, axis=1)
    start_jerk = jnp.take(jerk_old, active_stars, axis=1)
    change = start_accel - accel_now
    snap_term = -6.0 * change - step_time * (4.0 * start_jerk + 2.0 * jerk_now)
    crackle_term = 12.0 * change + 6.0 * step_time * (start_jerk + jerk_now)
    return (regular, irregular, jnp.concatenate([snap_term, crackle_term], axis=0))


def solution(mesh):
    in_specs = (
        P(None, ("blk", "grp")),
        P(None, ("blk", "grp")),
        P(None, ("blk", "grp")),
        P(None, ("blk", "grp")),
        P(("blk", "grp")),
        P(("blk", "grp")),
        P(("blk", "grp")),
        P(("blk", "grp"), None),
        P(("blk", "grp")),
    )
    out_specs = (P(None, ("blk", "grp")), P(None, ("blk", "grp")), P(None, ("blk", "grp")))
    return jax.shard_map(
        per_device, mesh=mesh, in_specs=in_specs, out_specs=out_specs, check_vma=False
    )
```

profile of v0, /device:TPU:0, one launch (start us, length us, event | category | flops | bytes accessed | tf_op | source)
XLA Modules:
  0.0 124.4 jit_solution(17634852802452686656)
XLA Ops:
  7.2 0.0 copy-start
  7.2 0.0 reduce-scatter.4.cloned.1.call-start
  7.2 0.7 broadcast_multiply_fusion
  7.9 0.7 multiply_add_fusion.1
  8.7 0.0 copy-start.5
  8.7 0.1 copy.181
  8.8 0.5 copy-done.5
  9.4 0.7 gather_fusion.2
  10.1 0.6 gather_fusion
  10.7 0.1 select_bitcast_fusion.2
  10.7 0.1 copy.182
  10.8 15.7 %all-gather.1 = f32[8,32,6]{1,2,0:T(8,128)S(1)} all-gather(f32[1,32,6]{1,2,0:T(8,128)S(1)} %copy.182), channel_id=1, replica_groups=mesh['blk'=4,'grp'=8] {'grp'}, dimensions={0}, use_global_device_ids=true | all-gather | bytes 6912 | tf_op jit(solution)/shard_map/all_gather | solution.py:60
  26.5 0.1 reshape.542
  26.6 1.5 %collective-permute-start.1 = (f32[6,256]{1,0:T(8,128)S(1)}, f32[6,256]{1,0:T(8,128)S(1)}, u32[]{:S(2)}, u32[]{:S(2)}) collective-permute-start(f32[6,256]{1,0:T(8,128)S(1)} %bitcast.128), channel_id=1, source_target_pairs={{24,0},{0,8},{8,16},{16,24},{25,1},{1,9},{9,17},{17,25},{26,2},{2,... | collective-permute-start | bytes 18440 | tf_op jit(solution)/shard_map/ppermute | solution.py:15
  28.7 0.0 copy-start.7
  28.7 0.6 copy-done.7
  29.4 0.6 dynamic-slice.5
  30.0 0.8 dynamic-update-slice
  30.7 8.9 %all-reduce = s32[8]{0:T(128)S(1)} all-reduce(s32[8]{0:T(128)S(1)} %dynamic-update-slice), channel_id=1, replica_groups=mesh['blk'=4,'grp'=8] {'grp'}, use_global_device_ids=true, to_apply=%add | all-reduce | flops 8 | bytes 64
  39.7 0.1 iota_compare_fusion
  39.7 0.7 copy-done.6
  40.4 9.2 %all-gather = s32[8,1,16]{2,1,0:T(1,128)S(1)} all-gather(s32[1,1,16]{2,1,0:T(1,128)S(1)} %bitcast.224), channel_id=1, replica_groups=mesh['blk'=4,'grp'=8] {'grp'}, dimensions={0}, use_global_device_ids=true | all-gather | bytes 576 | tf_op jit(solution)/shard_map/all_gather | solution.py:62
  49.6 0.2 and_reduce_fusion
  49.8 0.1 broadcast_in_dim.88
  49.9 0.1 reshape.491
  49.9 0.7 copy-done.4
  50.6 0.7 fusion.5
  51.4 1.5 %collective-permute-start = (f32[6,256]{1,0:T(8,128)S(1)}, f32[6,256]{1,0:T(8,128)S(1)}, u32[]{:S(2)}, u32[]{:S(2)}) collective-permute-start(f32[6,256]{1,0:T(8,128)S(1)} %stack.143), channel_id=1, source_target_pairs={{24,0},{0,8},{8,16},{16,24},{25,1},{1,9},{9,17},{17,25},{26,2},{2,... | collective-permute-start | bytes 18440 | tf_op jit(solution)/shard_map/ppermute | solution.py:15
  53.0 14.0 %all_gather.15 = f32[7,16,128]{2,0,1:T(8,128)S(1)} all-gather(f32[7,2,128]{2,0,1:T(8,128)S(1)} %pad_maximum_fusion.1), channel_id=1, replica_groups=mesh['blk'=4,'grp'=8] {'grp'}, dimensions={1}, use_global_device_ids=true | all-gather | bytes 64512 | tf_op jit(solution)/shard_map/all_gather | solution.py:101
  67.0 0.6 gather_fusion.1
  67.5 0.1 select_bitcast_fusion
  67.7 0.0 collective-permute-done.1
  67.7 1.5 %collective-permute-start.3 = (f32[6,256]{1,0:T(8,128)S(1)}, f32[6,256]{1,0:T(8,128)S(1)}, u32[]{:S(2)}, u32[]{:S(2)}) collective-permute-start(f32[6,256]{1,0:T(8,128)S(1)} %collective-permute-done.1), channel_id=1, source_target_pairs={{24,0},{0,8},{8,16},{16,24},{25,1},{1,9},{9,17},{17,25},{26,2},{2,... | collective-permute-start | bytes 18440 | tf_op jit(solution)/shard_map/ppermute | solution.py:15
  69.2 0.7 fusion.11
  70.0 0.0 collective-permute-done
  70.0 0.5 collective-permute-start.2
  70.5 1.7 %collective-permute-done.3 = f32[6,256]{1,0:T(8,128)S(1)} collective-permute-done((f32[6,256]{1,0:T(8,128)S(1)}, f32[6,256]{1,0:T(8,128)S(1)}, u32[]{:S(2)}, u32[]{:S(2)}) %collective-permute-start.3) | collective-permute-done | bytes 6176 | tf_op jit(solution)/shard_map/ppermute | solution.py:15
  72.3 0.6 collective-permute-start.5
  72.9 4.0 %collective-permute-done.5 = f32[6,256]{1,0:T(8,128)S(1)} collective-permute-done((f32[6,256]{1,0:T(8,128)S(1)}, f32[6,256]{1,0:T(8,128)S(1)}, u32[]{:S(2)}, u32[]{:S(2)}) %collective-permute-start.5) | collective-permute-done | bytes 6176 | tf_op jit(solution)/shard_map/ppermute | solution.py:15
  76.8 1.4 %fusion.23 = (f32[256]{0:T(256)S(1)}, f32[256]{0:T(256)S(1)}, f32[256]{0:T(256)S(1)}, f32[256]{0:T(256)S(1)}, f32[256]{0:T(256)S(1)}, /*index=5*/f32[256]{0:T(25...) fusion(f32[256]{0:T(256)S(1)} %bitcast.213, ...), kind=kLoop, calls=%fused_computation.108 | loop fusion | flops 5239808 | bytes 31744 | tf_op jit(solution)/shard_map/while/body/eval_jaxpr/reduce_sum | solution.py:37
  78.3 0.0 collective-permute-done.2
  78.3 0.1 collective-permute-start.4
  78.4 0.1 bitcast_multiply_fusion
  78.5 4.4 %collective-permute-done.4 = f32[6,256]{1,0:T(8,128)S(1)} collective-permute-done((f32[6,256]{1,0:T(8,128)S(1)}, f32[6,256]{1,0:T(8,128)S(1)}, u32[]{:S(2)}, u32[]{:S(2)}) %collective-permute-start.4) | collective-permute-done | bytes 6176 | tf_op jit(solution)/shard_map/ppermute | solution.py:15
  82.9 0.0 collective-permute-start.6
  82.9 0.3 slice_reduce_fusion.1
  83.2 4.3 %collective-permute-done.6 = f32[6,256]{1,0:T(8,128)S(1)} collective-permute-done((f32[6,256]{1,0:T(8,128)S(1)}, f32[6,256]{1,0:T(8,128)S(1)}, u32[]{:S(2)}, u32[]{:S(2)}) %collective-permute-start.6) | collective-permute-done | bytes 6176 | tf_op jit(solution)/shard_map/ppermute | solution.py:15
  87.5 0.8 copy.189
  88.2 0.0 reduce-scatter.4.cloned.1.call-update
  88.3 0.0 copy-start.2
  88.3 0.6 fusion.29
  88.9 0.1 copy-done.2
  89.0 0.1 copy.185
  89.1 0.5 copy-done.3
  89.6 0.1 copy.187
  89.8 0.6 gather_fusion.3
  90.4 0.1 copy.186
  90.4 0.6 gather_fusion.4
  91.0 0.1 copy.188
  91.1 0.6 stack.171
  91.7 23.8 %reduce-scatter.4.cloned.1.call-done = f32[32,6]{1,0:T(8,128)} async-done(((f32[256,6]{1,0:T(8,128)}), f32[32,6]{1,0:T(8,128)}) %reduce-scatter.4.cloned.1.call-update) | async-done | bytes 784
  115.5 0.8 copy.190
  116.3 0.6 copy-done.1
  116.9 0.6 pad_maximum_fusion.2
  (33 shorter events, 0.3 us)
Async XLA Ops:
  7.2 0.8 copy-start
  7.2 108.3 %reduce-scatter.4.cloned.1.call-start = ((), (), s32[]{:S(2)}) async-start(), calls=%async_computation.1 | async-start | bytes 147456
  8.7 0.7 copy-start.5
  26.6 41.1 %collective-permute-start.1 = (f32[6,256]{1,0:T(8,128)S(1)}, f32[6,256]{1,0:T(8,128)S(1)}, u32[]{:S(2)}, u32[]{:S(2)}) collective-permute-start(f32[6,256]{1,0:T(8,128)S(1)} %bitcast.128), channel_id=1, source_target_pairs={{24,0},{0,8},{8,16},{16,24},{25,1},{1,9},{9,17},{17,25},{26,2},{2,... | collective-permute-start | bytes 18440 | tf_op jit(solution)/shard_map/ppermute | solution.py:15
  28.7 0.7 copy-start.7
  39.7 0.7 copy-start.6
  49.9 0.7 copy-start.4
  51.4 18.6 %collective-permute-start = (f32[6,256]{1,0:T(8,128)S(1)}, f32[6,256]{1,0:T(8,128)S(1)}, u32[]{:S(2)}, u32[]{:S(2)}) collective-permute-start(f32[6,256]{1,0:T(8,128)S(1)} %stack.143), channel_id=1, source_target_pairs={{24,0},{0,8},{8,16},{16,24},{25,1},{1,9},{9,17},{17,25},{26,2},{2,... | collective-permute-start | bytes 18440 | tf_op jit(solution)/shard_map/ppermute | solution.py:15
  67.7 4.6 %collective-permute-start.3 = (f32[6,256]{1,0:T(8,128)S(1)}, f32[6,256]{1,0:T(8,128)S(1)}, u32[]{:S(2)}, u32[]{:S(2)}) collective-permute-start(f32[6,256]{1,0:T(8,128)S(1)} %collective-permute-done.1), channel_id=1, source_target_pairs={{24,0},{0,8},{8,16},{16,24},{25,1},{1,9},{9,17},{17,25},{26,2},{2,... | collective-permute-start | bytes 18440 | tf_op jit(solution)/shard_map/ppermute | solution.py:15
  70.0 8.3 %collective-permute-start.2 = (f32[6,256]{1,0:T(8,128)S(1)}, f32[6,256]{1,0:T(8,128)S(1)}, u32[]{:S(2)}, u32[]{:S(2)}) collective-permute-start(f32[6,256]{1,0:T(8,128)S(1)} %add.233), channel_id=1, source_target_pairs={{24,0},{0,8},{8,16},{16,24},{25,1},{1,9},{9,17},{17,25},{26,2},{2,... | collective-permute-start | bytes 18440 | tf_op jit(solution)/shard_map/ppermute | solution.py:15
  72.3 4.5 %collective-permute-start.5 = (f32[6,256]{1,0:T(8,128)S(1)}, f32[6,256]{1,0:T(8,128)S(1)}, u32[]{:S(2)}, u32[]{:S(2)}) collective-permute-start(f32[6,256]{1,0:T(8,128)S(1)} %collective-permute-done.3), channel_id=1, source_target_pairs={{24,0},{0,8},{8,16},{16,24},{25,1},{1,9},{9,17},{17,25},{26,2},{2,... | collective-permute-start | bytes 18440 | tf_op jit(solution)/shard_map/ppermute | solution.py:15
  78.3 4.6 %collective-permute-start.4 = (f32[6,256]{1,0:T(8,128)S(1)}, f32[6,256]{1,0:T(8,128)S(1)}, u32[]{:S(2)}, u32[]{:S(2)}) collective-permute-start(f32[6,256]{1,0:T(8,128)S(1)} %add.239), channel_id=1, source_target_pairs={{24,0},{0,8},{8,16},{16,24},{25,1},{1,9},{9,17},{17,25},{26,2},{2,... | collective-permute-start | bytes 18440 | tf_op jit(solution)/shard_map/ppermute | solution.py:15
  82.9 4.5 %collective-permute-start.6 = (f32[6,256]{1,0:T(8,128)S(1)}, f32[6,256]{1,0:T(8,128)S(1)}, u32[]{:S(2)}, u32[]{:S(2)}) collective-permute-start(f32[6,256]{1,0:T(8,128)S(1)} %add.245), channel_id=1, source_target_pairs={{24,0},{0,8},{8,16},{16,24},{25,1},{1,9},{9,17},{17,25},{26,2},{2,... | collective-permute-start | bytes 18440 | tf_op jit(solution)/shard_map/ppermute | solution.py:15
  88.3 0.7 copy-start.2
  89.0 0.7 copy-start.3
  116.3 0.6 copy-start.1
Sparse Core Ops, SparseCore 0:
  88.4 27.0 reduce-scatter.3
where the time goes:
time: 125 us; the launch traced here: 124 us
  blocking collectives  47.8 us (38%)
  waiting for transfers between devices  38.2 us (31%)
  between operations  14.9 us (12%)
  local copies, waits for them, and re-layouts  11.5 us (9%)
  other arithmetic  6.14 us (5%)
  starting transfers between devices  5.8 us (5%)
    unnamed x2, waiting for transfers between devices  23.8 us
    all_gather x1, blocking collectives, per_device(): group_set = lax.all_gather(own_set, 'grp', axis=1, tiled=True)  15.7 us
    ppermute x7, waiting for transfers between devices, shifted(): return lax.ppermute(block, axis, route)  14.4 us
    all_gather x1, blocking collectives, per_device(): everyone = lax.all_gather(block_data, 'grp', axis=1, tiled=True)  14 us
    all_gather x1, blocking collectives, per_device(): lax.all_gather(neighbour_list, 'grp', axis=0, tiled=True)  9.18 us
    unnamed x1, blocking collectives  8.93 us
    unnamed x25, local copies, waits for them, and re-layouts  7.03 us
    ppermute x7, starting transfers between devices, shifted(): return lax.ppermute(block, axis, route)  5.76 us
  transfers between devices with their start and end apart: 8, of which 5 were waited for; matrix products, arithmetic and copies ran while one was open for 7% of the time, Pallas kernels for 0%

commit v1 on v0

v1 whole, which is shorter than its diff:
```python
import functools

import jax
import jax.numpy as jnp
from jax import lax
from jax.experimental import pallas as pl
from jax.experimental.pallas import tpu as pltpu
from jax.sharding import PartitionSpec as P

BLOCK = 128
LANES = 128
SOFTEN_SQ = 0.0001
MESH = pl.DeviceIdType.MESH


def xor(a, b, size):
    out, bit = 0, 1
    while bit < size:
        out = out + ((a // bit + b // bit) % 2) * bit
        bit *= 2
    return out


def pair_terms(target, source):
    gap = [source[c] - target[c] for c in range(3)]
    rel = [source[c + 3] - target[c + 3] for c in range(3)]
    dist_sq = gap[0] * gap[0] + gap[1] * gap[1] + gap[2] * gap[2] + SOFTEN_SQ
    inverse = lax.rsqrt(dist_sq)
    inv_sq = inverse * inverse
    scaled = source[6] * (inv_sq * inverse)
    radial = 3.0 * (gap[0] * rel[0] + gap[1] * rel[1] + gap[2] * rel[2]) * inv_sq
    return [scaled * g for g in gap] + [
        scaled * (r - radial * g) for r, g in zip(rel, gap)
    ]


def kernel(
    n_blk, n_grp,
    pos, vel, acc, jerk, elapsed, masses, active, listing, count,
    regular, irregular, correction,
    src, tgt, spread, far, near, flags, columns, out_tx, out_rx,
    src_send, src_recv, tgt_send, tgt_recv, out_send, out_recv,
):
    blk, grp = lax.axis_index("blk"), lax.axis_index("grp")
    res_dev = pos.shape[1]
    act_dev = active.shape[1]
    blk_dev = res_dev // BLOCK
    per_pack = LANES // act_dev
    packs = n_blk // per_pack

    barrier = pltpu.get_barrier_semaphore()
    for k in range(1, n_grp):
        pl.semaphore_signal(
            barrier, inc=1, device_id=(blk, xor(grp, k, n_grp)), device_id_type=MESH
        )
    for k in range(1, n_blk):
        pl.semaphore_signal(
            barrier, inc=1, device_id=(xor(blk, k, n_blk), grp), device_id_type=MESH
        )

    t = elapsed[...]
    p, v, a, j = pos[...], vel[...], acc[...], jerk[...]
    src[0, 0:3, :] = p + t * (v + t * (0.5 * a + t * j / 6.0))
    src[0, 3:6, :] = v + t * (a + 0.5 * t * j)
    src[0, 6:7, :] = masses[...]
    src[0, 7:8, :] = t

    chosen = jnp.concatenate([active[...]] * per_pack, axis=1)
    chosen = jnp.broadcast_to(chosen, (8, LANES))
    place = chosen % BLOCK
    old = jnp.concatenate([a, j, t, t], axis=0)
    own_new = jnp.zeros((8, LANES), jnp.float32)
    own_old = jnp.zeros((8, LANES), jnp.float32)
    for b in range(blk_dev):
        here = chosen // BLOCK == b
        cut = slice(b * BLOCK, (b + 1) * BLOCK)
        own_new = jnp.where(
            here, jnp.take_along_axis(src[0, :, cut], place, axis=1), own_new
        )
        own_old = jnp.where(
            here, jnp.take_along_axis(old[:, cut], place, axis=1), own_old
        )
    tgt[0] = own_new

    pl.semaphore_wait(barrier, n_grp - 1 + n_blk - 1)

    def tgt_copy(k):
        return pltpu.make_async_remote_copy(
            src_ref=tgt.at[0], dst_ref=tgt.at[k],
            send_sem=tgt_send.at[k], recv_sem=tgt_recv.at[k],
            device_id=(xor(blk, k, n_blk), grp), device_id_type=MESH,
        )

    def src_copy(k):
        return pltpu.make_async_remote_copy(
            src_ref=src.at[0], dst_ref=src.at[k],
            send_sem=src_send.at[k], recv_sem=src_recv.at[k],
            device_id=(blk, xor(grp, k, n_grp)), device_id_type=MESH,
        )

    def out_copy(k):
        pack = k // per_pack
        return pltpu.make_async_remote_copy(
            src_ref=out_tx.at[pack], dst_ref=out_rx.at[k],
            send_sem=out_send.at[k], recv_sem=out_recv.at[k],
            device_id=(xor(blk, k, n_blk), grp), device_id_type=MESH,
        )

    for k in range(1, n_blk):
        tgt_copy(k).start()
    for k in reversed(range(1, n_grp)):
        src_copy(k).start()

    slots = listing.shape[1]
    names = lax.broadcasted_iota(jnp.int32, (blk_dev * n_grp, slots), 0)
    spots = lax.broadcasted_iota(jnp.int32, (blk_dev * n_grp, slots), 1)
    hit = (listing[...] == names) & (spots < count[...])
    member = jnp.max(jnp.where(hit, 1.0, 0.0), axis=1, keepdims=True)
    flags[...] = jnp.broadcast_to(member, flags.shape)

    for k in range(1, n_blk):
        tgt_copy(k).wait_recv()
    lane = lax.broadcasted_iota(jnp.int32, (8, LANES), 1)
    for pack in range(packs):
        mixed = tgt[pack * per_pack]
        for i in range(1, per_pack):
            mixed = jnp.where(lane >= i * act_dev, tgt[pack * per_pack + i], mixed)
        turned = mixed.T
        for c in range(6):
            spread[c, pack * LANES : (pack + 1) * LANES, :] = jnp.broadcast_to(
                turned[:, c : c + 1], (LANES, LANES)
            )

    def add_block(k, first):
        source = [
            [src[k, c : c + 1, b * BLOCK : (b + 1) * BLOCK] for c in range(7)]
            for b in range(blk_dev)
        ]

        def far_slot(slot, carry):
            rows = pl.ds(pl.multiple_of(slot * act_dev, act_dev), act_dev)
            target = [spread[c, rows, :] for c in range(6)]
            terms = pair_terms(target, source[0])
            for b in range(1, blk_dev):
                terms = [x + y for x, y in zip(terms, pair_terms(target, source[b]))]
            for c in range(6):
                far[c, rows, :] = terms[c] if first else far[c, rows, :] + terms[c]
            return carry

        rows = slice(0, act_dev)
        target = [spread[c, rows, :] for c in range(6)]
        far_sum = [0.0 if first else far[c, rows, :] for c in range(6)]
        near_sum = [0.0 if first else near[c] for c in range(6)]
        for b in range(blk_dev):
            block_id = xor(grp, k, n_grp) * blk_dev + b
            is_near = flags[pl.ds(block_id, 1), :]
            for c, term in enumerate(pair_terms(target, source[b])):
                kept = term * is_near
                near_sum[c] = near_sum[c] + kept
                far_sum[c] = far_sum[c] + (term - kept)
        for c in range(6):
            far[c, rows, :] = far_sum[c]
            near[c] = near_sum[c]
        lax.fori_loop(1, n_blk, far_slot, 0)

    add_block(0, True)

    def later(k, carry):
        src_copy(k).wait_recv()
        add_block(k, False)
        return carry

    lax.fori_loop(1, n_grp, later, 0)

    for pack in range(packs):
        rows = slice(pack * LANES, (pack + 1) * LANES)
        lanes = lax.broadcasted_iota(jnp.int32, (LANES, LANES), 1)
        packed = jnp.zeros((LANES, LANES), jnp.float32)
        for c in range(6):
            total = jnp.sum(far[c, rows, :], axis=1, keepdims=True)
            packed = jnp.where(lanes == c, total, packed)
        columns[...] = packed
        if pack == 0:
            mine = columns[0:act_dev, :]
            for c in range(6):
                total = jnp.sum(near[c], axis=1, keepdims=True)
                mine = jnp.where(lanes[:act_dev] == c + 8, total, mine)
            columns[0:act_dev, :] = mine
        flat = columns[...].T
        out_tx[pack] = flat[0:8, :]
        if pack == 0:
            irr = flat[8:14, 0:act_dev]
        for k in range(max(1, pack * per_pack), (pack + 1) * per_pack):
            out_copy(k).start()

    reg = out_tx[0][0:6, 0:act_dev]
    irregular[...] = irr
    for k in range(1, n_blk):
        out_copy(k).wait_recv()
        left = (k % per_pack) * act_dev
        reg = reg + out_rx[k][0:6, left : left + act_dev]
    regular[...] = reg
    total = reg + irr
    accel_now, jerk_now = total[0:3], total[3:6]
    mine = own_old[:, 0:act_dev]
    start_accel, start_jerk, step = mine[0:3], mine[3:6], mine[6:7]
    change = start_accel - accel_now
    correction[0:3, :] = -6.0 * change - step * (4.0 * start_jerk + 2.0 * jerk_now)
    correction[3:6, :] = 12.0 * change + 6.0 * step * (start_jerk + jerk_now)

    for k in range(1, n_blk):
        tgt_copy(k).wait_send()
        out_copy(k).wait_send()
    for k in range(1, n_grp):
        src_copy(k).wait_send()


def per_device(
    n_blk, n_grp,
    position, velocity, accel_old, jerk_old, elapsed, masses,
    active_stars, neighbour_list, neighbour_count,
):
    act_dev = active_stars.shape[0]
    res_dev = position.shape[1]
    packs = n_blk * act_dev // LANES
    shape = jax.ShapeDtypeStruct((6, act_dev), jnp.float32)
    vmem = pl.BlockSpec(memory_space=pltpu.VMEM)
    f32 = jnp.float32
    return pl.pallas_call(
        functools.partial(kernel, n_blk, n_grp),
        out_shape=(shape, shape, shape),
        in_specs=[vmem] * 9,
        out_specs=(vmem, vmem, vmem),
        scratch_shapes=[
            pltpu.VMEM((n_grp, 8, res_dev), f32),
            pltpu.VMEM((n_blk, 8, LANES), f32),
            pltpu.VMEM((6, packs * LANES, LANES), f32),
            pltpu.VMEM((6, packs * LANES, LANES), f32),
            pltpu.VMEM((6, act_dev, LANES), f32),
            pltpu.VMEM((n_grp * res_dev // BLOCK, LANES), f32),
            pltpu.VMEM((LANES, LANES), f32),
            pltpu.VMEM((packs, 8, LANES), f32),
            pltpu.VMEM((n_blk, 8, LANES), f32),
            pltpu.SemaphoreType.DMA((n_grp,)),
            pltpu.SemaphoreType.DMA((n_grp,)),
            pltpu.SemaphoreType.DMA((n_blk,)),
            pltpu.SemaphoreType.DMA((n_blk,)),
            pltpu.SemaphoreType.DMA((n_blk,)),
            pltpu.SemaphoreType.DMA((n_blk,)),
        ],
        compiler_params=pltpu.CompilerParams(collective_id=0, has_side_effects=True),
        cost_estimate=pl.CostEstimate(
            flops=40 * n_blk * act_dev * n_grp * res_dev,
            bytes_accessed=32 * res_dev * n_grp,
            transcendentals=n_blk * act_dev * n_grp * res_dev,
        ),
    )(
        position, velocity, accel_old, jerk_old,
        elapsed.reshape(1, -1), masses.reshape(1, -1), active_stars.reshape(1, -1),
        neighbour_list, neighbour_count.reshape(1, -1),
    )


def solution(mesh):
    stars = P(None, ("blk", "grp"))
    flat = P(("blk", "grp"))
    return jax.shard_map(
        functools.partial(per_device, mesh.shape["blk"], mesh.shape["grp"]),
        mesh=mesh,
        in_specs=(stars,) * 4 + (flat,) * 3 + (P(("blk", "grp"), None), flat),
        out_specs=(stars,) * 3,
        check_vma=False,
    )
```

time: 125 us -> 19.8 us (0.16)
  blocking collectives: 47.8 us -> 0 us
  waiting for transfers between devices: 38.2 us -> 0 us
  Pallas kernels: 0 us -> 15.5 us
  between operations: 14.9 us -> 1.3 us
  local copies, waits for them, and re-layouts: 11.5 us -> 2.62 us
  other arithmetic: 6.14 us -> 0 us
  starting transfers between devices: 5.8 us -> 0 us
    all_gather x3 -> x0, blocking collectives: 38.8 us -> none  [the longest x1 15.7 us: per_device(): group_set = lax.all_gather(own_set, 'grp', axis=1, tiled=True)]
    unnamed x2 -> x0, waiting for transfers between devices: 23.8 us -> none
    pallas_call x0 -> x1, Pallas kernels: none -> 15.5 us  [per_device(): pl.pallas_call(functools.partial(kernel, n_blk, n_grp), out_shape=(shape,...]
    ppermute x7 -> x0, waiting for transfers between devices: 14.4 us -> none  [shifted(): return lax.ppermute(block, axis, route)]
    unnamed x1 -> x0, blocking collectives: 8.93 us -> none
    ppermute x7 -> x0, starting transfers between devices: 5.76 us -> none  [shifted(): return lax.ppermute(block, axis, route)]
    unnamed x25 -> x9, local copies, waits for them, and re-layouts: 7.03 us -> 2.62 us
    reduce_sum x4 -> x0, other arithmetic: 3.47 us -> none  [pair_sums(): return jnp.stack([jnp.sum(scaled * term, axis=1) for term in term_list])]
  transfers between devices with their start and end apart: 8 -> 0, of which waited for: 5 -> 0; matrix products, arithmetic and copies ran while one was open for 7% -> 0% of each run, Pallas kernels for 0% -> 0%
where the time goes in v1:
time: 19.8 us; the launch traced here: 19.5 us
  Pallas kernels  15.5 us (78%)
  local copies, waits for them, and re-layouts  2.62 us (13%)
  between operations  1.3 us (7%)
    pallas_call x1, Pallas kernels, per_device(): pl.pallas_call(functools.partial(kernel, n_blk, n_grp), out_shape=(shape,...  15.5 us
    unnamed x9, local copies, waits for them, and re-layouts  2.62 us

profile of v1, /device:TPU:0, one launch (start us, length us, event | category | flops | bytes accessed | tf_op | source)
XLA Modules:
  0.0 19.5 jit_solution(1224447949827544799)
XLA Ops:
  1.3 15.5 %shard_map.112 = (f32[6,32]{1,0:T(8,128)}, f32[6,32]{1,0:T(8,128)}, f32[6,32]{1,0:T(8,128)}) custom-call(f32[3,256]{1,0:T(4,128)} %pos.1, f32[3,256]{1,0:T(4,128)} %vel.1, f32[3,256]{1,0:T(4,128)} %acc.1, f32[3,256]{1,0:T(4,128)} %jerk.1, f32[1,256]{1,0:T(1,128)} %bitcast.5, f32[1,256]{1,0:T(1,128)} %bitcast.6, s32[1,32]{1,0:T(1,128)} %bitcast.7, ...), custom_call_target="tpu_custom_call" | custom-call | flops 10485760 | bytes 65536 | tf_op jit(solution)/shard_map/pallas_call | solution.py:229
  16.8 0.0 copy-start.2
  16.8 0.7 %copy-done.2 = f32[6,32]{1,0:T(8,128)S(1)} copy-done((f32[6,32]{1,0:T(8,128)S(1)}, f32[6,32]{1,0:T(8,128)}, u32[]{:S(2)}) %copy-start.2) | copy-done | bytes 792
  17.5 0.0 copy-start.1
  17.5 0.6 %copy.16 = f32[6,32]{1,0:T(8,128)} copy(f32[6,32]{1,0:T(8,128)S(1)} %copy-done.2) | data formatting | bytes 1536
  18.1 0.1 copy-done.1
  18.2 0.0 copy-start
  18.2 0.6 %copy.17 = f32[6,32]{1,0:T(8,128)} copy(f32[6,32]{1,0:T(8,128)S(1)} %copy-done.1) | data formatting | bytes 1536
  18.8 0.1 copy-done
  18.9 0.6 %copy.18 = f32[6,32]{1,0:T(8,128)} copy(f32[6,32]{1,0:T(8,128)S(1)} %copy-done) | data formatting | bytes 1536
Async XLA Ops:
  16.8 0.7 %copy-start.2 = (f32[6,32]{1,0:T(8,128)S(1)}, f32[6,32]{1,0:T(8,128)}, u32[]{:S(2)}) copy-start(f32[6,32]{1,0:T(8,128)} %get-tuple-element.6) | copy-start | bytes 2308
  17.5 0.7 %copy-start.1 = (f32[6,32]{1,0:T(8,128)S(1)}, f32[6,32]{1,0:T(8,128)}, u32[]{:S(2)}) copy-start(f32[6,32]{1,0:T(8,128)} %get-tuple-element.7) | copy-start | bytes 2308
  18.2 0.7 %copy-start = (f32[6,32]{1,0:T(8,128)S(1)}, f32[6,32]{1,0:T(8,128)}, u32[]{:S(2)}) copy-start(f32[6,32]{1,0:T(8,128)} %get-tuple-element.8) | copy-start | bytes 2308

commit v2 on v1

--- a/solution.py
+++ b/solution.py
@@ -36,8 +36,9 @@
 
 def kernel(
     n_blk, n_grp,
-    pos, vel, acc, jerk, elapsed, masses, active, listing, count,
-    regular, irregular, correction,
+    pos_hbm, vel_hbm, acc_hbm, jerk_hbm, elapsed_hbm, masses_hbm, active_hbm,
+    listing_hbm, count_hbm, result,
+    pos, vel, acc, jerk, elapsed, masses, active, listing, count, in_sem,
     src, tgt, spread, far, near, flags, columns, out_tx, out_rx,
     src_send, src_recv, tgt_send, tgt_recv, out_send, out_recv,
 ):
@@ -58,6 +59,20 @@
             barrier, inc=1, device_id=(xor(blk, k, n_blk), grp), device_id_type=MESH
         )
 
+    loads = [
+        pltpu.make_async_copy(there, here, in_sem.at[i])
+        for i, (there, here) in enumerate(
+            (
+                (pos_hbm, pos), (vel_hbm, vel), (acc_hbm, acc), (jerk_hbm, jerk),
+                (elapsed_hbm, elapsed), (masses_hbm, masses), (active_hbm, active),
+                (listing_hbm, listing), (count_hbm, count),
+            )
+        )
+    ]
+    for load in loads:
+        load.start()
+    for load in loads:
+        load.wait()
     t = elapsed[...]
     p, v, a, j = pos[...], vel[...], acc[...], jerk[...]
     src[0, 0:3, :] = p + t * (v + t * (0.5 * a + t * j / 6.0))
@@ -114,7 +129,7 @@
     slots = listing.shape[1]
     names = lax.broadcasted_iota(jnp.int32, (blk_dev * n_grp, slots), 0)
     spots = lax.broadcasted_iota(jnp.int32, (blk_dev * n_grp, slots), 1)
-    hit = (listing[...] == names) & (spots < count[...])
+    hit = (listing[...] == names) & (spots < count[0])
     member = jnp.max(jnp.where(hit, 1.0, 0.0), axis=1, keepdims=True)
     flags[...] = jnp.broadcast_to(member, flags.shape)
 
@@ -194,25 +209,32 @@
             out_copy(k).start()
 
     reg = out_tx[0][0:6, 0:act_dev]
-    irregular[...] = irr
+    result[8:14, 0:act_dev] = irr
     for k in range(1, n_blk):
         out_copy(k).wait_recv()
         left = (k % per_pack) * act_dev
         reg = reg + out_rx[k][0:6, left : left + act_dev]
-    regular[...] = reg
+    result[0:6, 0:act_dev] = reg
     total = reg + irr
     accel_now, jerk_now = total[0:3], total[3:6]
     mine = own_old[:, 0:act_dev]
     start_accel, start_jerk, step = mine[0:3], mine[3:6], mine[6:7]
     change = start_accel - accel_now
-    correction[0:3, :] = -6.0 * change - step * (4.0 * start_jerk + 2.0 * jerk_now)
-    correction[3:6, :] = 12.0 * change + 6.0 * step * (start_jerk + jerk_now)
+    result[16:19, 0:act_dev] = -6.0 * change - step * (4.0 * start_jerk + 2.0 * jerk_now)
+    result[19:22, 0:act_dev] = 12.0 * change + 6.0 * step * (start_jerk + jerk_now)
 
     for k in range(1, n_blk):
         tgt_copy(k).wait_send()
         out_copy(k).wait_send()
     for k in range(1, n_grp):
         src_copy(k).wait_send()
+
+
+def write_out(result, regular, irregular, correction):
+    act_dev = regular.shape[1]
+    regular[...] = result[0:6, 0:act_dev]
+    irregular[...] = result[8:14, 0:act_dev]
+    correction[...] = result[16:22, 0:act_dev]
 
 
 def per_device(
@@ -226,12 +248,22 @@
     shape = jax.ShapeDtypeStruct((6, act_dev), jnp.float32)
     vmem = pl.BlockSpec(memory_space=pltpu.VMEM)
     f32 = jnp.float32
-    return pl.pallas_call(
+    result = pl.pallas_call(
         functools.partial(kernel, n_blk, n_grp),
-        out_shape=(shape, shape, shape),
-        in_specs=[vmem] * 9,
-        out_specs=(vmem, vmem, vmem),
+        out_shape=pltpu.VMEM((24, LANES), f32),
+        in_specs=[pl.BlockSpec(memory_space=pltpu.HBM)] * 9,
+        out_specs=vmem,
         scratch_shapes=[
+            pltpu.VMEM(position.shape, f32),
+            pltpu.VMEM(position.shape, f32),
+            pltpu.VMEM(position.shape, f32),
+            pltpu.VMEM(position.shape, f32),
+            pltpu.VMEM((1, res_dev), f32),
+            pltpu.VMEM((1, res_dev), f32),
+            pltpu.VMEM((1, act_dev), jnp.int32),
+            pltpu.VMEM(neighbour_list.shape, jnp.int32),
+            pltpu.SMEM((1,), jnp.int32),
+            pltpu.SemaphoreType.DMA((9,)),
             pltpu.VMEM((n_grp, 8, res_dev), f32),
             pltpu.VMEM((n_blk, 8, LANES), f32),
             pltpu.VMEM((6, packs * LANES, LANES), f32),
@@ -257,8 +289,14 @@
     )(
         position, velocity, accel_old, jerk_old,
         elapsed.reshape(1, -1), masses.reshape(1, -1), active_stars.reshape(1, -1),
-        neighbour_list, neighbour_count.reshape(1, -1),
+        neighbour_list, neighbour_count,
     )
+    return pl.pallas_call(
+        write_out,
+        out_shape=(shape, shape, shape),
+        in_specs=[vmem],
+        out_specs=(vmem, vmem, vmem),
+    )(result)
 
 
 def solution(mesh):

time: 19.8 us -> 17.9 us (0.904)
  local copies, waits for them, and re-layouts: 2.62 us -> 0.59 us
  Pallas kernels: 15.5 us -> 15.7 us
    unnamed x9 -> x2, local copies, waits for them, and re-layouts: 2.62 us -> 0.59 us
    pallas_call x1 -> x2, Pallas kernels: 15.5 us -> 15.7 us  [the longest x1 14.3 us: per_device(): pl.pallas_call(functools.partial(kernel, n_blk, n_grp), out_shape=pltpu.V...]
where the time goes in v2:
time: 17.9 us; the launch traced here: 17.5 us
  Pallas kernels  15.7 us (88%)
  between operations  1.3 us (7%)
  local copies, waits for them, and re-layouts  0.59 us (3%)
    pallas_call x1, Pallas kernels, per_device(): pl.pallas_call(functools.partial(kernel, n_blk, n_grp), out_shape=pltpu.V...  14.3 us
    pallas_call x1, Pallas kernels, per_device(): pl.pallas_call(write_out, out_shape=(shape, shape, shape), in_specs=[vmem...  1.31 us
    unnamed x2, local copies, waits for them, and re-layouts  0.59 us

profile of v2, /device:TPU:0, one launch (start us, length us, event | category | flops | bytes accessed | tf_op | source)
XLA Modules:
  0.0 17.5 jit_solution(13718915149832962346)
XLA Ops:
  1.3 14.3 %shard_map.112.result = f32[24,128]{1,0:T(8,128)S(1)} custom-call(f32[3,256]{1,0:T(4,128)} %pos_hbm.1, f32[3,256]{1,0:T(4,128)} %vel_hbm.1, f32[3,256]{1,0:T(4,128)} %acc_hbm.1, f32[3,256]{1,0:T(4,128)} %jerk_hbm.1, f32[1,256]{1,0:T(1,128)} %bitcast.3, f32[1,256]{1,0:T(1,128)} %bitcast.4, s32[1,32]{1,0:T(1,128)} %bitcast.5, s32[1,16]{1,0:T(1,128)} %listing_hbm.1, ...), custom_call_target="tpu_custom_call" | custom-call | flops 10485760 | bytes 65536 | tf_op jit(solution)/shard_map/pallas_call | solution.py:251
  15.6 0.0 copy-start
  15.6 0.6 %copy-done = f32[24,128]{1,0:T(8,128)} copy-done((f32[24,128]{1,0:T(8,128)}, f32[24,128]{1,0:T(8,128)S(1)}, u32[]{:S(2)}) %copy-start) | copy-done | bytes 12312
  16.2 1.3 %shard_map.113 = (f32[6,32]{1,0:T(8,128)}, f32[6,32]{1,0:T(8,128)}, f32[6,32]{1,0:T(8,128)}) custom-call(f32[24,128]{1,0:T(8,128)} %copy-done), custom_call_target="tpu_custom_call" | custom-call | tf_op jit(solution)/shard_map/pallas_call | solution.py:294
Async XLA Ops:
  15.6 0.6 %copy-start = (f32[24,128]{1,0:T(8,128)}, f32[24,128]{1,0:T(8,128)S(1)}, u32[]{:S(2)}) copy-start(f32[24,128]{1,0:T(8,128)S(1)} %shard_map.112.result) | copy-start | bytes 36868

commit v3 on v2

--- a/solution.py
+++ b/solution.py
@@ -28,7 +28,7 @@
     inverse = lax.rsqrt(dist_sq)
     inv_sq = inverse * inverse
     scaled = source[6] * (inv_sq * inverse)
-    radial = 3.0 * (gap[0] * rel[0] + gap[1] * rel[1] + gap[2] * rel[2]) * inv_sq
+    radial = (gap[0] * rel[0] + gap[1] * rel[1] + gap[2] * rel[2]) * (3.0 * inv_sq)
     return [scaled * g for g in gap] + [
         scaled * (r - radial * g) for r, g in zip(rel, gap)
     ]
@@ -176,7 +176,7 @@
         for c in range(6):
             far[c, rows, :] = far_sum[c]
             near[c] = near_sum[c]
-        lax.fori_loop(1, n_blk, far_slot, 0)
+        lax.fori_loop(1, n_blk, far_slot, 0, unroll=True)
 
     add_block(0, True)
 
@@ -296,7 +296,7 @@
         out_shape=(shape, shape, shape),
         in_specs=[vmem],
         out_specs=(vmem, vmem, vmem),
-    )(result)
+    )(pltpu.with_memory_space_constraint(result, pltpu.VMEM))
 
 
 def solution(mesh):

time: 17.9 us -> 16.2 us (0.905)
  Pallas kernels: 15.7 us -> 14.7 us
  local copies, waits for them, and re-layouts: 0.59 us -> 0 us
    pallas_call x1, Pallas kernels: 1.31 us -> 0.6 us  [per_device(): pl.pallas_call(write_out, out_shape=(shape, shape, shape), in_specs=[vmem...]
    unnamed x2 -> x0, local copies, waits for them, and re-layouts: 0.59 us -> none
    pallas_call x1, Pallas kernels: 14.3 us -> 14.1 us  [per_device(): pl.pallas_call(functools.partial(kernel, n_blk, n_grp), out_shape=pltpu.V...]
where the time goes in v3:
time: 16.2 us; the launch traced here: 16 us
  Pallas kernels  14.7 us (91%)
  between operations  1.29 us (8%)
    pallas_call x1, Pallas kernels, per_device(): pl.pallas_call(functools.partial(kernel, n_blk, n_grp), out_shape=pltpu.V...  14.1 us
    pallas_call x1, Pallas kernels, per_device(): pl.pallas_call(write_out, out_shape=(shape, shape, shape), in_specs=[vmem...  0.6 us

profile of v3, /device:TPU:0, one launch (start us, length us, event | category | flops | bytes accessed | tf_op | source)
XLA Modules:
  0.0 16.0 jit_solution(14073504861486813198)
XLA Ops:
  1.3 14.1 %shard_map.112.result = f32[24,128]{1,0:T(8,128)S(1)} custom-call(f32[3,256]{1,0:T(4,128)} %pos_hbm.1, f32[3,256]{1,0:T(4,128)} %vel_hbm.1, f32[3,256]{1,0:T(4,128)} %acc_hbm.1, f32[3,256]{1,0:T(4,128)} %jerk_hbm.1, f32[1,256]{1,0:T(1,128)} %bitcast.3, f32[1,256]{1,0:T(1,128)} %bitcast.4, s32[1,32]{1,0:T(1,128)} %bitcast.5, s32[1,16]{1,0:T(1,128)} %listing_hbm.1, ...), custom_call_target="tpu_custom_call" | custom-call | flops 10485760 | bytes 65536 | tf_op jit(solution)/shard_map/pallas_call | solution.py:251
  15.4 0.6 %shard_map.113 = (f32[6,32]{1,0:T(8,128)}, f32[6,32]{1,0:T(8,128)}, f32[6,32]{1,0:T(8,128)}) custom-call(f32[24,128]{1,0:T(8,128)S(1)} %shard_map.112.result), custom_call_target="tpu_custom_call" | custom-call | tf_op jit(solution)/shard_map/pallas_call | solution.py:294

commit v4 on v3

--- a/solution.py
+++ b/solution.py
@@ -39,7 +39,7 @@
     pos_hbm, vel_hbm, acc_hbm, jerk_hbm, elapsed_hbm, masses_hbm, active_hbm,
     listing_hbm, count_hbm, result,
     pos, vel, acc, jerk, elapsed, masses, active, listing, count, in_sem,
-    src, tgt, spread, far, near, flags, columns, out_tx, out_rx,
+    src, tgt, spread, far, near, flags, out_tx, out_rx,
     src_send, src_recv, tgt_send, tgt_recv, out_send, out_recv,
 ):
     blk, grp = lax.axis_index("blk"), lax.axis_index("grp")
@@ -96,6 +96,8 @@
             here, jnp.take_along_axis(old[:, cut], place, axis=1), own_old
         )
     tgt[0] = own_new
+    far[...] = jnp.zeros_like(far)
+    near[...] = jnp.zeros_like(near)
 
     pl.semaphore_wait(barrier, n_grp - 1 + n_blk - 1)
 
@@ -146,69 +148,79 @@
                 turned[:, c : c + 1], (LANES, LANES)
             )
 
-    def add_block(k, first):
-        source = [
+    def block_slot(i):
+        before = i - 1
+        other = before + (before + n_grp - grp) // n_grp
+        return jnp.where(i == 0, 0, xor(grp, other, n_grp))
+
+    def source_rows(k):
+        return [
             [src[k, c : c + 1, b * BLOCK : (b + 1) * BLOCK] for c in range(7)]
             for b in range(blk_dev)
         ]
 
-        def far_slot(slot, carry):
-            rows = pl.ds(pl.multiple_of(slot * act_dev, act_dev), act_dev)
+    def add_others(i, carry):
+        k = block_slot(i)
+
+        @pl.when(i > 0)
+        def _():
+            src_copy(k).wait_recv()
+
+        source = source_rows(k)
+        for slot in range(1, n_blk):
+            rows = slice(slot * act_dev, (slot + 1) * act_dev)
             target = [spread[c, rows, :] for c in range(6)]
             terms = pair_terms(target, source[0])
             for b in range(1, blk_dev):
                 terms = [x + y for x, y in zip(terms, pair_terms(target, source[b]))]
             for c in range(6):
-                far[c, rows, :] = terms[c] if first else far[c, rows, :] + terms[c]
-            return carry
-
-        rows = slice(0, act_dev)
-        target = [spread[c, rows, :] for c in range(6)]
-        far_sum = [0.0 if first else far[c, rows, :] for c in range(6)]
-        near_sum = [0.0 if first else near[c] for c in range(6)]
-        for b in range(blk_dev):
-            block_id = xor(grp, k, n_grp) * blk_dev + b
-            is_near = flags[pl.ds(block_id, 1), :]
-            for c, term in enumerate(pair_terms(target, source[b])):
-                kept = term * is_near
-                near_sum[c] = near_sum[c] + kept
-                far_sum[c] = far_sum[c] + (term - kept)
-        for c in range(6):
-            far[c, rows, :] = far_sum[c]
-            near[c] = near_sum[c]
-        lax.fori_loop(1, n_blk, far_slot, 0, unroll=True)
-
-    add_block(0, True)
-
-    def later(k, carry):
-        src_copy(k).wait_recv()
-        add_block(k, False)
+                far[c, rows, :] = far[c, rows, :] + terms[c]
         return carry
 
-    lax.fori_loop(1, n_grp, later, 0)
-
+    lax.fori_loop(0, n_grp, add_others, 0)
+
+    lanes = lax.broadcasted_iota(jnp.int32, (LANES, LANES), 1)
     for pack in range(packs):
         rows = slice(pack * LANES, (pack + 1) * LANES)
-        lanes = lax.broadcasted_iota(jnp.int32, (LANES, LANES), 1)
         packed = jnp.zeros((LANES, LANES), jnp.float32)
         for c in range(6):
             total = jnp.sum(far[c, rows, :], axis=1, keepdims=True)
             packed = jnp.where(lanes == c, total, packed)
-        columns[...] = packed
-        if pack == 0:
-            mine = columns[0:act_dev, :]
-            for c in range(6):
-                total = jnp.sum(near[c], axis=1, keepdims=True)
-                mine = jnp.where(lanes[:act_dev] == c + 8, total, mine)
-            columns[0:act_dev, :] = mine
-        flat = columns[...].T
-        out_tx[pack] = flat[0:8, :]
-        if pack == 0:
-            irr = flat[8:14, 0:act_dev]
+        out_tx[pack] = packed.T[0:8, :]
         for k in range(max(1, pack * per_pack), (pack + 1) * per_pack):
             out_copy(k).start()
 
-    reg = out_tx[0][0:6, 0:act_dev]
+    own = slice(0, act_dev)
+
+    def add_own(i, carry):
+        target = [spread[c, own, :] for c in range(6)]
+        far_sum = [far[c, own, :] for c in range(6)]
+        near_sum = [near[c] for c in range(6)]
+        for k in (2 * i, 2 * i + 1):
+            source = source_rows(k)
+            for b in range(blk_dev):
+                block_id = xor(grp, k, n_grp) * blk_dev + b
+                is_near = flags[pl.ds(block_id, 1), :]
+                for c, term in enumerate(pair_terms(target, source[b])):
+                    kept = term * is_near
+                    near_sum[c] = near_sum[c] + kept
+                    far_sum[c] = far_sum[c] + (term - kept)
+        for c in range(6):
+            far[c, own, :] = far_sum[c]
+            near[c] = near_sum[c]
+        return carry
+
+    lax.fori_loop(0, n_grp // 2, add_own, 0)
+
+    packed = jnp.zeros((act_dev, LANES), jnp.float32)
+    for c in range(6):
+        total = jnp.sum(far[c, own, :], axis=1, keepdims=True)
+        packed = jnp.where(lanes[:act_dev] == c, total, packed)
+        total = jnp.sum(near[c], axis=1, keepdims=True)
+        packed = jnp.where(lanes[:act_dev] == c + 8, total, packed)
+    flat = packed.T
+    reg, irr = flat[0:6, :], flat[8:14, :]
+
     result[8:14, 0:act_dev] = irr
     for k in range(1, n_blk):
         out_copy(k).wait_recv()
@@ -270,7 +282,6 @@
             pltpu.VMEM((6, packs * LANES, LANES), f32),
             pltpu.VMEM((6, act_dev, LANES), f32),
             pltpu.VMEM((n_grp * res_dev // BLOCK, LANES), f32),
-            pltpu.VMEM((LANES, LANES), f32),
             pltpu.VMEM((packs, 8, LANES), f32),
             pltpu.VMEM((n_blk, 8, LANES), f32),
             pltpu.SemaphoreType.DMA((n_grp,)),

time: 16.2 us -> 15.9 us (0.981)
  Pallas kernels: 14.7 us -> 14.4 us
    pallas_call x1, Pallas kernels: 14.1 us -> 13.8 us  [per_device(): pl.pallas_call(functools.partial(kernel, n_blk, n_grp), out_shape=pltpu.V...]
where the time goes in v4:
time: 15.9 us; the launch traced here: 15.7 us
  Pallas kernels  14.4 us (91%)
  between operations  1.29 us (8%)
    pallas_call x1, Pallas kernels, per_device(): pl.pallas_call(functools.partial(kernel, n_blk, n_grp), out_shape=pltpu.V...  13.8 us
    pallas_call x1, Pallas kernels, per_device(): pl.pallas_call(write_out, out_shape=(shape, shape, shape), in_specs=[vmem...  0.6 us

profile of v4, /device:TPU:0, one launch (start us, length us, event | category | flops | bytes accessed | tf_op | source)
XLA Modules:
  0.0 15.7 jit_solution(534273109878865248)
XLA Ops:
  1.3 13.8 %shard_map.112.result = f32[24,128]{1,0:T(8,128)S(1)} custom-call(f32[3,256]{1,0:T(4,128)} %pos_hbm.1, f32[3,256]{1,0:T(4,128)} %vel_hbm.1, f32[3,256]{1,0:T(4,128)} %acc_hbm.1, f32[3,256]{1,0:T(4,128)} %jerk_hbm.1, f32[1,256]{1,0:T(1,128)} %bitcast.3, f32[1,256]{1,0:T(1,128)} %bitcast.4, s32[1,32]{1,0:T(1,128)} %bitcast.5, s32[1,16]{1,0:T(1,128)} %listing_hbm.1, ...), custom_call_target="tpu_custom_call" | custom-call | flops 10485760 | bytes 65536 | tf_op jit(solution)/shard_map/pallas_call | solution.py:263
  15.1 0.6 %shard_map.113 = (f32[6,32]{1,0:T(8,128)}, f32[6,32]{1,0:T(8,128)}, f32[6,32]{1,0:T(8,128)}) custom-call(f32[24,128]{1,0:T(8,128)S(1)} %shard_map.112.result), custom_call_target="tpu_custom_call" | custom-call | tf_op jit(solution)/shard_map/pallas_call | solution.py:305

commit v5 on v4

--- a/solution.py
+++ b/solution.py
@@ -50,7 +50,7 @@
     packs = n_blk // per_pack
 
     barrier = pltpu.get_barrier_semaphore()
-    for k in range(1, n_grp):
+    for k in [1, *range(2, n_grp, 2)]:
         pl.semaphore_signal(
             barrier, inc=1, device_id=(blk, xor(grp, k, n_grp)), device_id_type=MESH
         )
@@ -99,7 +99,7 @@
     far[...] = jnp.zeros_like(far)
     near[...] = jnp.zeros_like(near)
 
-    pl.semaphore_wait(barrier, n_grp - 1 + n_blk - 1)
+    pl.semaphore_wait(barrier, n_grp // 2 + n_blk - 1)
 
     def tgt_copy(k):
         return pltpu.make_async_remote_copy(
@@ -113,6 +113,13 @@
             src_ref=src.at[0], dst_ref=src.at[k],
             send_sem=src_send.at[k], recv_sem=src_recv.at[k],
             device_id=(blk, xor(grp, k, n_grp)), device_id_type=MESH,
+        )
+
+    def hand_on(k):
+        return pltpu.make_async_remote_copy(
+            src_ref=src.at[k], dst_ref=src.at[k + 1],
+            send_sem=src_send.at[k + 1], recv_sem=src_recv.at[k + 1],
+            device_id=(blk, xor(grp, 1, n_grp)), device_id_type=MESH,
         )
 
     def out_copy(k):
@@ -125,8 +132,9 @@
 
     for k in range(1, n_blk):
         tgt_copy(k).start()
-    for k in reversed(range(1, n_grp)):
+    for k in reversed(range(2, n_grp, 2)):
         src_copy(k).start()
+    hand_on(0).start()
 
     slots = listing.shape[1]
     names = lax.broadcasted_iota(jnp.int32, (blk_dev * n_grp, slots), 0)
@@ -148,36 +156,42 @@
                 turned[:, c : c + 1], (LANES, LANES)
             )
 
-    def block_slot(i):
-        before = i - 1
-        other = before + (before + n_grp - grp) // n_grp
-        return jnp.where(i == 0, 0, xor(grp, other, n_grp))
-
     def source_rows(k):
         return [
-            [src[k, c : c + 1, b * BLOCK : (b + 1) * BLOCK] for c in range(7)]
+            [
+                jnp.broadcast_to(
+                    src[k, c : c + 1, b * BLOCK : (b + 1) * BLOCK], (8, LANES)
+                )
+                for c in range(7)
+            ]
             for b in range(blk_dev)
         ]
 
-    def add_others(i, carry):
-        k = block_slot(i)
-
-        @pl.when(i > 0)
-        def _():
-            src_copy(k).wait_recv()
-
+    def add_others(k):
         source = source_rows(k)
-        for slot in range(1, n_blk):
-            rows = slice(slot * act_dev, (slot + 1) * act_dev)
+        for low in range(act_dev, n_blk * act_dev, 8):
+            rows = slice(low, low + 8)
             target = [spread[c, rows, :] for c in range(6)]
             terms = pair_terms(target, source[0])
             for b in range(1, blk_dev):
                 terms = [x + y for x, y in zip(terms, pair_terms(target, source[b]))]
             for c in range(6):
                 far[c, rows, :] = far[c, rows, :] + terms[c]
+
+    def two_devices(i, carry):
+        k = 2 * i
+
+        @pl.when(i > 0)
+        def _():
+            src_copy(k).wait_recv()
+            hand_on(k).start()
+
+        add_others(k)
+        hand_on(k).wait_recv()
+        add_others(k + 1)
         return carry
 
-    lax.fori_loop(0, n_grp, add_others, 0)
+    lax.fori_loop(0, n_grp // 2, two_devices, 0)
 
     lanes = lax.broadcasted_iota(jnp.int32, (LANES, LANES), 1)
     for pack in range(packs):
@@ -192,25 +206,28 @@
 
     own = slice(0, act_dev)
 
-    def add_own(i, carry):
-        target = [spread[c, own, :] for c in range(6)]
-        far_sum = [far[c, own, :] for c in range(6)]
-        near_sum = [near[c] for c in range(6)]
-        for k in (2 * i, 2 * i + 1):
-            source = source_rows(k)
+    def add_own(k, carry):
+        source = source_rows(k)
+        is_near = []
+        for b in range(blk_dev):
+            block_id = xor(grp, k, n_grp) * blk_dev + b
+            is_near.append(jnp.broadcast_to(flags[pl.ds(block_id, 1), :], (8, LANES)))
+        for low in range(0, act_dev, 8):
+            rows = slice(low, low + 8)
+            target = [spread[c, rows, :] for c in range(6)]
+            far_sum = [far[c, rows, :] for c in range(6)]
+            near_sum = [near[c, rows, :] for c in range(6)]
             for b in range(blk_dev):
-                block_id = xor(grp, k, n_grp) * blk_dev + b
-                is_near = flags[pl.ds(block_id, 1), :]
                 for c, term in enumerate(pair_terms(target, source[b])):
-                    kept = term * is_near
+                    kept = term * is_near[b]
                     near_sum[c] = near_sum[c] + kept
                     far_sum[c] = far_sum[c] + (term - kept)
-        for c in range(6):
-            far[c, own, :] = far_sum[c]
-            near[c] = near_sum[c]
+            for c in range(6):
+                far[c, rows, :] = far_sum[c]
+                near[c, rows, :] = near_sum[c]
         return carry
 
-    lax.fori_loop(0, n_grp // 2, add_own, 0)
+    lax.fori_loop(0, n_grp, add_own, 0)
 
     packed = jnp.zeros((act_dev, LANES), jnp.float32)
     for c in range(6):
@@ -238,7 +255,9 @@
     for k in range(1, n_blk):
         tgt_copy(k).wait_send()
         out_copy(k).wait_send()
-    for k in range(1, n_grp):
+    for k in range(0, n_grp, 2):
+        hand_on(k).wait_send()
+    for k in range(2, n_grp, 2):
         src_copy(k).wait_send()
 
 

time: 15.9 us -> 17.3 us (1.088)
  Pallas kernels: 14.4 us -> 15.8 us
    pallas_call x1, Pallas kernels: 13.8 us -> 15.2 us  [per_device(): pl.pallas_call(functools.partial(kernel, n_blk, n_grp), out_shape=pltpu.V...]
where the time goes in v5:
time: 17.3 us; the launch traced here: 17.1 us
  Pallas kernels  15.8 us (91%)
  between operations  1.29 us (7%)
    pallas_call x1, Pallas kernels, per_device(): pl.pallas_call(functools.partial(kernel, n_blk, n_grp), out_shape=pltpu.V...  15.2 us
    pallas_call x1, Pallas kernels, per_device(): pl.pallas_call(write_out, out_shape=(shape, shape, shape), in_specs=[vmem...  0.6 us

profile of v5, /device:TPU:0, one launch (start us, length us, event | category | flops | bytes accessed | tf_op | source)
XLA Modules:
  0.0 17.1 jit_solution(5760763096320937530)
XLA Ops:
  1.3 15.2 %shard_map.112.result = f32[24,128]{1,0:T(8,128)S(1)} custom-call(f32[3,256]{1,0:T(4,128)} %pos_hbm.1, f32[3,256]{1,0:T(4,128)} %vel_hbm.1, f32[3,256]{1,0:T(4,128)} %acc_hbm.1, f32[3,256]{1,0:T(4,128)} %jerk_hbm.1, f32[1,256]{1,0:T(1,128)} %bitcast.3, f32[1,256]{1,0:T(1,128)} %bitcast.4, s32[1,32]{1,0:T(1,128)} %bitcast.5, s32[1,16]{1,0:T(1,128)} %listing_hbm.1, ...), custom_call_target="tpu_custom_call" | custom-call | flops 10485760 | bytes 65536 | tf_op jit(solution)/shard_map/pallas_call | solution.py:282
  16.5 0.6 %shard_map.113 = (f32[6,32]{1,0:T(8,128)}, f32[6,32]{1,0:T(8,128)}, f32[6,32]{1,0:T(8,128)}) custom-call(f32[24,128]{1,0:T(8,128)S(1)} %shard_map.112.result), custom_call_target="tpu_custom_call" | custom-call | tf_op jit(solution)/shard_map/pallas_call | solution.py:324

commit v6 on v5

--- a/solution.py
+++ b/solution.py
@@ -160,7 +160,7 @@
         return [
             [
                 jnp.broadcast_to(
-                    src[k, c : c + 1, b * BLOCK : (b + 1) * BLOCK], (8, LANES)
+                    src[k, c : c + 1, b * BLOCK : (b + 1) * BLOCK], (act_dev, LANES)
                 )
                 for c in range(7)
             ]
@@ -169,8 +169,8 @@
 
     def add_others(k):
         source = source_rows(k)
-        for low in range(act_dev, n_blk * act_dev, 8):
-            rows = slice(low, low + 8)
+        for low in range(act_dev, n_blk * act_dev, act_dev):
+            rows = slice(low, low + act_dev)
             target = [spread[c, rows, :] for c in range(6)]
             terms = pair_terms(target, source[0])
             for b in range(1, blk_dev):
@@ -211,9 +211,9 @@
         is_near = []
         for b in range(blk_dev):
             block_id = xor(grp, k, n_grp) * blk_dev + b
-            is_near.append(jnp.broadcast_to(flags[pl.ds(block_id, 1), :], (8, LANES)))
-        for low in range(0, act_dev, 8):
-            rows = slice(low, low + 8)
+            is_near.append(jnp.broadcast_to(flags[pl.ds(block_id, 1), :], (act_dev, LANES)))
+        for low in range(0, act_dev, act_dev):
+            rows = slice(low, low + act_dev)
             target = [spread[c, rows, :] for c in range(6)]
             far_sum = [far[c, rows, :] for c in range(6)]
             near_sum = [near[c, rows, :] for c in range(6)]

time: 17.3 us -> 17.3 us (level)
  no operation moved by 1% of the time
where the time goes in v6:
time: 17.3 us; the launch traced here: 17 us
  Pallas kernels  15.8 us (91%)
  between operations  1.29 us (7%)
    pallas_call x1, Pallas kernels, per_device(): pl.pallas_call(functools.partial(kernel, n_blk, n_grp), out_shape=pltpu.V...  15.2 us
    pallas_call x1, Pallas kernels, per_device(): pl.pallas_call(write_out, out_shape=(shape, shape, shape), in_specs=[vmem...  0.6 us

profile of v6, /device:TPU:0, one launch (start us, length us, event | category | flops | bytes accessed | tf_op | source)
XLA Modules:
  0.0 17.0 jit_solution(1699493894083519593)
XLA Ops:
  1.3 15.2 %shard_map.112.result = f32[24,128]{1,0:T(8,128)S(1)} custom-call(f32[3,256]{1,0:T(4,128)} %pos_hbm.1, f32[3,256]{1,0:T(4,128)} %vel_hbm.1, f32[3,256]{1,0:T(4,128)} %acc_hbm.1, f32[3,256]{1,0:T(4,128)} %jerk_hbm.1, f32[1,256]{1,0:T(1,128)} %bitcast.3, f32[1,256]{1,0:T(1,128)} %bitcast.4, s32[1,32]{1,0:T(1,128)} %bitcast.5, s32[1,16]{1,0:T(1,128)} %listing_hbm.1, ...), custom_call_target="tpu_custom_call" | custom-call | flops 10485760 | bytes 65536 | tf_op jit(solution)/shard_map/pallas_call | solution.py:282
  16.4 0.6 %shard_map.113 = (f32[6,32]{1,0:T(8,128)}, f32[6,32]{1,0:T(8,128)}, f32[6,32]{1,0:T(8,128)}) custom-call(f32[24,128]{1,0:T(8,128)S(1)} %shard_map.112.result), custom_call_target="tpu_custom_call" | custom-call | tf_op jit(solution)/shard_map/pallas_call | solution.py:324

commit v7 on v4

--- a/solution.py
+++ b/solution.py
@@ -148,21 +148,14 @@
                 turned[:, c : c + 1], (LANES, LANES)
             )
 
-    def block_slot(i):
-        before = i - 1
-        other = before + (before + n_grp - grp) // n_grp
-        return jnp.where(i == 0, 0, xor(grp, other, n_grp))
-
     def source_rows(k):
         return [
             [src[k, c : c + 1, b * BLOCK : (b + 1) * BLOCK] for c in range(7)]
             for b in range(blk_dev)
         ]
 
-    def add_others(i, carry):
-        k = block_slot(i)
-
-        @pl.when(i > 0)
+    def add_others(k, carry):
+        @pl.when(k > 0)
         def _():
             src_copy(k).wait_recv()
 

time: 15.9 us -> 15.7 us (0.987)
  Pallas kernels: 14.4 us -> 14.2 us
    pallas_call x1, Pallas kernels: 13.8 us -> 13.6 us  [per_device(): pl.pallas_call(functools.partial(kernel, n_blk, n_grp), out_shape=pltpu.V...]
where the time goes in v7:
time: 15.7 us; the launch traced here: 15.5 us
  Pallas kernels  14.2 us (90%)
  between operations  1.29 us (8%)
    pallas_call x1, Pallas kernels, per_device(): pl.pallas_call(functools.partial(kernel, n_blk, n_grp), out_shape=pltpu.V...  13.6 us
    pallas_call x1, Pallas kernels, per_device(): pl.pallas_call(write_out, out_shape=(shape, shape, shape), in_specs=[vmem...  0.6 us

profile of v7, /device:TPU:0, one launch (start us, length us, event | category | flops | bytes accessed | tf_op | source)
XLA Modules:
  0.0 15.5 jit_solution(17283877941998134843)
XLA Ops:
  1.3 13.6 %shard_map.112.result = f32[24,128]{1,0:T(8,128)S(1)} custom-call(f32[3,256]{1,0:T(4,128)} %pos_hbm.1, f32[3,256]{1,0:T(4,128)} %vel_hbm.1, f32[3,256]{1,0:T(4,128)} %acc_hbm.1, f32[3,256]{1,0:T(4,128)} %jerk_hbm.1, f32[1,256]{1,0:T(1,128)} %bitcast.3, f32[1,256]{1,0:T(1,128)} %bitcast.4, s32[1,32]{1,0:T(1,128)} %bitcast.5, s32[1,16]{1,0:T(1,128)} %listing_hbm.1, ...), custom_call_target="tpu_custom_call" | custom-call | flops 10485760 | bytes 65536 | tf_op jit(solution)/shard_map/pallas_call | solution.py:256
  14.9 0.6 %shard_map.113 = (f32[6,32]{1,0:T(8,128)}, f32[6,32]{1,0:T(8,128)}, f32[6,32]{1,0:T(8,128)}) custom-call(f32[24,128]{1,0:T(8,128)S(1)} %shard_map.112.result), custom_call_target="tpu_custom_call" | custom-call | tf_op jit(solution)/shard_map/pallas_call | solution.py:298

commit v8 on v7

--- a/solution.py
+++ b/solution.py
@@ -125,7 +125,7 @@
 
     for k in range(1, n_blk):
         tgt_copy(k).start()
-    for k in reversed(range(1, n_grp)):
+    for k in range(1, n_grp):
         src_copy(k).start()
 
     slots = listing.shape[1]

time: 15.7 us -> 15.7 us (level)
  no operation moved by 1% of the time
where the time goes in v8:
time: 15.7 us; the launch traced here: 15.5 us
  Pallas kernels  14.2 us (90%)
  between operations  1.29 us (8%)
    pallas_call x1, Pallas kernels, per_device(): pl.pallas_call(functools.partial(kernel, n_blk, n_grp), out_shape=pltpu.V...  13.6 us
    pallas_call x1, Pallas kernels, per_device(): pl.pallas_call(write_out, out_shape=(shape, shape, shape), in_specs=[vmem...  0.6 us

profile of v8, /device:TPU:0, one launch (start us, length us, event | category | flops | bytes accessed | tf_op | source)
XLA Modules:
  0.0 15.5 jit_solution(9738243169696427619)
XLA Ops:
  1.3 13.6 %shard_map.112.result = f32[24,128]{1,0:T(8,128)S(1)} custom-call(f32[3,256]{1,0:T(4,128)} %pos_hbm.1, f32[3,256]{1,0:T(4,128)} %vel_hbm.1, f32[3,256]{1,0:T(4,128)} %acc_hbm.1, f32[3,256]{1,0:T(4,128)} %jerk_hbm.1, f32[1,256]{1,0:T(1,128)} %bitcast.3, f32[1,256]{1,0:T(1,128)} %bitcast.4, s32[1,32]{1,0:T(1,128)} %bitcast.5, s32[1,16]{1,0:T(1,128)} %listing_hbm.1, ...), custom_call_target="tpu_custom_call" | custom-call | flops 10485760 | bytes 65536 | tf_op jit(solution)/shard_map/pallas_call | solution.py:256
  14.9 0.6 %shard_map.113 = (f32[6,32]{1,0:T(8,128)}, f32[6,32]{1,0:T(8,128)}, f32[6,32]{1,0:T(8,128)}) custom-call(f32[24,128]{1,0:T(8,128)S(1)} %shard_map.112.result), custom_call_target="tpu_custom_call" | custom-call | tf_op jit(solution)/shard_map/pallas_call | solution.py:298
